TPU v7x, 1024 devices: a whole 4x8x16 slice. The times are simulated.
1024 devices in a mesh: ctx: 128 (over z, y), dp: 8 (over x, core).
Axes of the slice: x: 4, y: 8, z: 16, core: 2. Of those that a mesh axis runs over, the one named last changes fastest.
Arguments:
- queries: bfloat16 [131072, 1536], P(('dp', 'ctx')), parts along dimension 0, may hold values from -8 to 8
- latents: bfloat16 [131072, 576], P(('dp', 'ctx')), parts along dimension 0, may hold values from -8 to 8
- key_up: bfloat16 [512, 1024], replicated, may hold values from -0.25 to 0.25
- value_up: bfloat16 [512, 1024], replicated, may hold values from -0.25 to 0.25
- link_mask: int32 [1024, 128], P(('dp', 'ctx')), parts along dimension 0, may hold values from 0 to 1, as said below
- out_grad: bfloat16 [131072, 1024], P(('dp', 'ctx')), parts along dimension 0, may hold values from -6 to 6
Outputs:
- attention: bfloat16 [131072, 1024], P(('dp', 'ctx')), parts along dimension 0
- grad_queries: bfloat16 [131072, 1536], P(('dp', 'ctx')), parts along dimension 0
- grad_latents: bfloat16 [131072, 576], P(('dp', 'ctx')), parts along dimension 0
There are 8 independent parts, one for each index of `dp`. A program takes and returns all parts, laid end to end along the dimension named above; an argument that names none is the same for every part. Nothing has to cross between parts.
Inputs may be any that keep to these rules, and one draw needn't show every extreme that they name: Entries are 0 or 1. link_mask[b, b] = 1, link_mask[b, b - 1] = 1 for b >= 1; any other 1 lies at c = b - 2 ** k for some k >= 1 with c >= 0. Each row holds at most 4 ones, and the last row exactly 4.
All inputs are finite; a program needn't handle non-finite values.
Results may differ from a plain program's by a relative error of at most 0.017.
Values may be sent and summed in bfloat16 or wider, within the bound.
A program may use at most 64 MiB of HBM per device.

v0:
```python
import jax
import jax.numpy as jnp
from jax import lax
from jax.sharding import PartitionSpec as P

HEADS = 8
NOPE = 128
ROPE = 64
LATENT = 512
LINK_MOST = 4


def passed_along(shard, axis, by):
    size = lax.axis_size(axis)
    pairs = [(i, i + by) for i in range(size) if 0 <= i + by < size]
    return lax.ppermute(shard, axis, pairs)


def on_device(queries, latents, key_up, value_up, link_mask, out_grad):
    devices = lax.axis_size("ctx")
    levels = devices.bit_length() - 1
    position = lax.axis_index("ctx")
    row_count = queries.shape[0]
    scale = (NOPE + ROPE) ** (-0.5)
    width_heads = HEADS * NOPE
    shaped = queries.reshape(row_count, HEADS, NOPE + ROPE)
    q_nope = shaped[:, :, :NOPE]
    q_rope = shaped[:, :, NOPE:]
    grad_out = out_grad.reshape(row_count, HEADS, NOPE)
    token_ids = jnp.arange(row_count)
    causal = token_ids[:, None] >= token_ids[None, :]
    flags = [link_mask[0, position] == 1]
    for level in range(levels):
        source = position - 2**level
        flags.append((source >= 0) & (link_mask[0, jnp.maximum(source, 0)] == 1))
    valid = jnp.stack(flags)
    fetched = [latents]
    for level in range(levels):
        fetched.append(passed_along(latents, "ctx", 2**level))
    candidates = jnp.stack(fetched)
    order = jnp.argsort(jnp.where(valid, 0, 1).astype(jnp.int32), stable=True)[:LINK_MOST]
    live = valid[order]
    is_diag = order == 0
    kv_slots = candidates[order]
    plain = kv_slots[:, :, :LATENT].reshape(LINK_MOST * row_count, LATENT)
    keys_nope = (
        jnp.dot(plain, key_up, preferred_element_type=jnp.float32)
        .astype(jnp.bfloat16)
        .reshape(LINK_MOST, row_count, HEADS, NOPE)
    )
    values = (
        jnp.dot(plain, value_up, preferred_element_type=jnp.float32)
        .astype(jnp.bfloat16)
        .reshape(LINK_MOST, row_count, HEADS, NOPE)
    )
    rope = kv_slots[:, :, LATENT:]
    scores = (
        jnp.einsum("thd,jshd->hjts", q_nope, keys_nope, preferred_element_type=jnp.float32)
        + jnp.einsum("thd,jsd->hjts", q_rope, rope, preferred_element_type=jnp.float32)
    ) * scale
    allowed = live[None, :, None, None] & (
        (~is_diag)[None, :, None, None] | causal[None, None, :, :]
    )
    scores = jnp.where(allowed, scores, -jnp.inf)
    peak = jnp.max(scores, axis=(1, 3), keepdims=True)
    powers = jnp.exp(scores - peak)
    probs = powers / jnp.sum(powers, axis=(1, 3), keepdims=True)
    probs_bf = probs.astype(jnp.bfloat16)
    attention = (
        jnp.einsum("hjts,jshd->thd", probs_bf, values, preferred_element_type=jnp.float32)
        .astype(jnp.bfloat16)
        .reshape(row_count, width_heads)
    )
    dprobs = jnp.einsum("thd,jshd->hjts", grad_out, values, preferred_element_type=jnp.float32)
    delta = jnp.sum(probs * dprobs, axis=(1, 3), keepdims=True)
    dscores = (probs * (dprobs - delta) * scale).astype(jnp.bfloat16)
    dq_nope = jnp.einsum("hjts,jshd->thd", dscores, keys_nope, preferred_element_type=jnp.float32)
    dq_rope = jnp.einsum("hjts,jsd->thd", dscores, rope, preferred_element_type=jnp.float32)
    grad_queries = (
        jnp.concatenate([dq_nope, dq_rope], axis=2)
        .astype(jnp.bfloat16)
        .reshape(row_count, HEADS * (NOPE + ROPE))
    )
    pair_keys = (
        jnp.einsum("hjts,thd->jshd", dscores, q_nope, preferred_element_type=jnp.float32)
        .astype(jnp.bfloat16)
        .reshape(LINK_MOST, row_count, width_heads)
    )
    pair_values = (
        jnp.einsum("hjts,thd->jshd", probs_bf, grad_out, preferred_element_type=jnp.float32)
        .astype(jnp.bfloat16)
        .reshape(LINK_MOST, row_count, width_heads)
    )
    pair_rope = jnp.einsum(
        "hjts,thd->jsd", dscores, q_rope, preferred_element_type=jnp.float32
    ).astype(jnp.bfloat16)
    flat_keys = pair_keys.reshape(LINK_MOST * row_count, width_heads)
    flat_values = pair_values.reshape(LINK_MOST * row_count, width_heads)
    grad_plain = jnp.dot(flat_keys, key_up.T, preferred_element_type=jnp.float32) + jnp.dot(
        flat_values, value_up.T, preferred_element_type=jnp.float32
    )
    share = jnp.concatenate(
        [grad_plain.reshape(LINK_MOST, row_count, LATENT), pair_rope.astype(jnp.float32)], axis=2
    )
    latent_sum = share[0]
    for level in range(1, levels + 1):
        weight = ((order == level) & live).astype(jnp.float32)
        piece = jnp.tensordot(weight, share, axes=1)
        latent_sum = latent_sum + passed_along(piece, "ctx", -(2 ** (level - 1)))
    grad_latents = latent_sum.astype(jnp.bfloat16)
    return (attention, grad_queries, grad_latents)


def solution(mesh):
    placed = (
        P(("dp", "ctx"), None),
        P(("dp", "ctx"), None),
        P(),
        P(),
        P(("dp", "ctx"), None),
        P(("dp", "ctx"), None),
    )
    return jax.shard_map(
        on_device,
        mesh=mesh,
        in_specs=placed,
        out_specs=(P(("dp", "ctx"), None), P(("dp", "ctx"), None), P(("dp", "ctx"), None)),
        check_vma=False,
    )
```

profile of v0, /device:TPU:507, one launch (start us, length us, event | category | flops | bytes accessed | tf_op | source)
XLA Modules:
  0.0 193.6 jit_solution(16811726854161285927)
XLA Ops:
  0.7 4.5 %collective-permute-start = (bf16[128,576]{0,1:T(8,128)(2,1)}, bf16[128,576]{0,1:T(8,128)(2,1)}, u32[]{:S(2)}, u32[]{:S(2)}) collective-permute-start(bf16[128,576]{0,1:T(8,128)(2,1)} %param.7), channel_id=1, source_target_pairs={{0,8},{8,16},{16,24},{24,32},{32,40},{40,48},{48,56},{56,64},{64,7... | collective-permute-start | bytes 442376 | tf_op jit(solution)/shard_map/ppermute | solution.py:16
  5.2 4.2 %collective-permute-start.1 = (bf16[128,576]{0,1:T(8,128)(2,1)}, bf16[128,576]{0,1:T(8,128)(2,1)S(1)}, u32[]{:S(2)}, u32[]{:S(2)}) collective-permute-start(bf16[128,576]{0,1:T(8,128)(2,1)} %param.7), channel_id=1, source_target_pairs={{0,16},{8,24},{16,32},{24,40},{32,48},{40,56},{48,64},{56,72},{64,... | collective-permute-start | bytes 442376 | tf_op jit(solution)/shard_map/ppermute | solution.py:16
  9.4 5.7 %collective-permute-start.2 = (bf16[128,576]{0,1:T(8,128)(2,1)}, bf16[128,576]{0,1:T(8,128)(2,1)S(1)}, u32[]{:S(2)}, u32[]{:S(2)}) collective-permute-start(bf16[128,576]{0,1:T(8,128)(2,1)} %param.7), channel_id=1, source_target_pairs={{0,32},{8,40},{16,48},{24,56},{32,64},{40,72},{48,80},{56,88},{64,... | collective-permute-start | bytes 442376 | tf_op jit(solution)/shard_map/ppermute | solution.py:16
  15.1 3.1 %collective-permute-start.3 = (bf16[128,576]{0,1:T(8,128)(2,1)}, bf16[128,576]{0,1:T(8,128)(2,1)S(1)}, u32[]{:S(2)}, u32[]{:S(2)}) collective-permute-start(bf16[128,576]{0,1:T(8,128)(2,1)} %param.7), channel_id=1, source_target_pairs={{0,64},{8,72},{16,80},{24,88},{32,96},{40,104},{48,112},{56,120},{... | collective-permute-start | bytes 442376 | tf_op jit(solution)/shard_map/ppermute | solution.py:16
  18.2 4.0 %collective-permute-start.4 = (bf16[128,576]{0,1:T(8,128)(2,1)}, bf16[128,576]{0,1:T(8,128)(2,1)S(1)}, u32[]{:S(2)}, u32[]{:S(2)}) collective-permute-start(bf16[128,576]{0,1:T(8,128)(2,1)} %param.7), channel_id=1, source_target_pairs={{0,128},{8,136},{16,144},{24,152},{32,160},{40,168},{48,176},{56,1... | collective-permute-start | bytes 442376 | tf_op jit(solution)/shard_map/ppermute | solution.py:16
  22.2 0.9 bitcast_dynamic-update-slice_fusion.7
  23.2 1.6 constant_dynamic-slice_fusion
  30.0 1.0 sort.17
  31.0 1.2 copy.26
  32.9 1.7 copy.71
  35.3 5.8 %collective-permute-start.5 = (bf16[128,576]{0,1:T(8,128)(2,1)S(1)}, bf16[128,576]{0,1:T(8,128)(2,1)S(1)}, u32[]{:S(2)}, u32[]{:S(2)}) collective-permute-start(bf16[128,576]{0,1:T(8,128)(2,1)S(1)} %copy-done.9), channel_id=1, source_target_pairs={{0,256},{8,264},{16,272},{24,280},{32,288},{40,296},{48,304},{56,3... | collective-permute-start | bytes 442376 | tf_op jit(solution)/shard_map/ppermute | solution.py:16
  41.1 0.9 bitcast_dynamic-update-slice_fusion.6
  42.1 1.3 collective-permute-start.6
  43.5 19.1 %collective-permute-done.5 = bf16[128,576]{0,1:T(8,128)(2,1)S(1)} collective-permute-done((bf16[128,576]{0,1:T(8,128)(2,1)S(1)}, bf16[128,576]{0,1:T(8,128)(2,1)S(1)}, u32[]{:S(2)}, u32[]{:S(2)}) %collective-permute-start.5) | collective-permute-done | bytes 147488 | tf_op jit(solution)/shard_map/ppermute | solution.py:16
  63.7 1.9 %fusion.10 = bf16[64,8,8,128]{3,1,2,0:T(8,128)(2,1)S(1)} fusion(bf16[512,512]{1,0:T(8,128)(2,1)S(1)} %bitcast.218, bf16[512,1024]{1,0:T(8,128)(2,1)} %param.9), kind=kOutput, calls=%fused_computation.23 | convolution fusion | flops 537395200 | bytes 2621440 | tf_op jit(solution)/shard_map/dot_general | solution.py:52
  65.6 1.2 copy.69
  67.9 1.0 copy.34
  69.8 1.4 fusion.100
  71.5 0.9 copy-done.4
  72.4 1.4 fusion.12
  75.1 1.1 fusion.18
  79.3 1.7 convolution_add_fusion
  81.0 1.6 copy.41
  82.7 1.3 fusion.29
  83.9 1.3 fusion.31
  85.2 1.3 fusion.33
  86.4 1.3 fusion.35
  87.7 1.3 fusion.37
  89.0 1.2 fusion.39
  90.2 1.3 collective-permute-start.13
  91.5 1.9 collective-permute-start.12
  93.5 1.3 fusion.41
  95.6 2.5 %collective-permute-start.11 = (f32[128,576]{0,1:T(8,128)}, f32[128,576]{0,1:T(8,128)}, u32[]{:S(2)}, u32[]{:S(2)}) collective-permute-start(f32[128,576]{0,1:T(8,128)} %bitcast.226), channel_id=1, source_target_pairs={{128,0},{136,8},{144,16},{152,24},{160,32},{168,40},{176,48},{184,... | collective-permute-start | bytes 884744 | tf_op jit(solution)/shard_map/ppermute | solution.py:16
  98.1 5.7 %collective-permute-start.10 = (f32[128,576]{0,1:T(8,128)}, f32[128,576]{0,1:T(8,128)}, u32[]{:S(2)}, u32[]{:S(2)}) collective-permute-start(f32[128,576]{0,1:T(8,128)} %bitcast.225), channel_id=1, source_target_pairs={{64,0},{72,8},{80,16},{88,24},{96,32},{104,40},{112,48},{120,56},{... | collective-permute-start | bytes 884744 | tf_op jit(solution)/shard_map/ppermute | solution.py:16
  103.7 3.5 %collective-permute-start.9 = (f32[128,576]{0,1:T(8,128)}, f32[128,576]{0,1:T(8,128)}, u32[]{:S(2)}, u32[]{:S(2)}) collective-permute-start(f32[128,576]{0,1:T(8,128)} %bitcast.224), channel_id=1, source_target_pairs={{32,0},{40,8},{48,16},{56,24},{64,32},{72,40},{80,48},{88,56},{96,... | collective-permute-start | bytes 884744 | tf_op jit(solution)/shard_map/ppermute | solution.py:16
  107.3 1.6 fusion.14
  108.9 1.1 collective-permute-done.13
  110.1 3.7 %collective-permute-start.8 = (f32[128,576]{0,1:T(8,128)}, f32[128,576]{0,1:T(8,128)}, u32[]{:S(2)}, u32[]{:S(2)}) collective-permute-start(f32[128,576]{0,1:T(8,128)} %bitcast.56), channel_id=1, source_target_pairs={{16,0},{24,8},{32,16},{40,24},{48,32},{56,40},{64,48},{72,56},{80,... | collective-permute-start | bytes 884744 | tf_op jit(solution)/shard_map/ppermute | solution.py:16
  113.8 22.9 %collective-permute-done.12 = f32[128,576]{0,1:T(8,128)} collective-permute-done((f32[128,576]{0,1:T(8,128)}, f32[128,576]{0,1:T(8,128)}, u32[]{:S(2)}, u32[]{:S(2)}) %collective-permute-start.12) | collective-permute-done | bytes 294944 | tf_op jit(solution)/shard_map/ppermute | solution.py:16
  136.7 2.9 %collective-permute-start.7 = (f32[128,576]{0,1:T(8,128)}, f32[128,576]{0,1:T(8,128)}, u32[]{:S(2)}, u32[]{:S(2)}) collective-permute-start(f32[128,576]{0,1:T(8,128)} %bitcast.54), channel_id=1, source_target_pairs={{8,0},{16,8},{24,16},{32,24},{40,32},{48,40},{56,48},{64,56},{72,6... | collective-permute-start | bytes 884744 | tf_op jit(solution)/shard_map/ppermute | solution.py:16
  139.6 1.1 fusion.16
  140.8 0.9 copy.43
  141.7 11.9 %collective-permute-done.11 = f32[128,576]{0,1:T(8,128)} collective-permute-done((f32[128,576]{0,1:T(8,128)}, f32[128,576]{0,1:T(8,128)}, u32[]{:S(2)}, u32[]{:S(2)}) %collective-permute-start.11) | collective-permute-done | bytes 294944 | tf_op jit(solution)/shard_map/ppermute | solution.py:16
  153.6 6.9 %collective-permute-done.10 = f32[128,576]{0,1:T(8,128)} collective-permute-done((f32[128,576]{0,1:T(8,128)}, f32[128,576]{0,1:T(8,128)}, u32[]{:S(2)}, u32[]{:S(2)}) %collective-permute-start.10) | collective-permute-done | bytes 294944 | tf_op jit(solution)/shard_map/ppermute | solution.py:16
  160.5 18.2 %collective-permute-done.9 = f32[128,576]{0,1:T(8,128)} collective-permute-done((f32[128,576]{0,1:T(8,128)}, f32[128,576]{0,1:T(8,128)}, u32[]{:S(2)}, u32[]{:S(2)}) %collective-permute-start.9) | collective-permute-done | bytes 294944 | tf_op jit(solution)/shard_map/ppermute | solution.py:16
  178.7 8.2 %collective-permute-done.8 = f32[128,576]{0,1:T(8,128)} collective-permute-done((f32[128,576]{0,1:T(8,128)}, f32[128,576]{0,1:T(8,128)}, u32[]{:S(2)}, u32[]{:S(2)}) %collective-permute-start.8) | collective-permute-done | bytes 294944 | tf_op jit(solution)/shard_map/ppermute | solution.py:16
  186.9 4.5 %collective-permute-done.7 = f32[128,576]{0,1:T(8,128)} collective-permute-done((f32[128,576]{0,1:T(8,128)}, f32[128,576]{0,1:T(8,128)}, u32[]{:S(2)}, u32[]{:S(2)}) %collective-permute-start.7) | collective-permute-done | bytes 294944 | tf_op jit(solution)/shard_map/ppermute | solution.py:16
  191.4 2.3 %fusion.52 = bf16[128,576]{0,1:T(8,128)(2,1)} fusion(f32[128,576]{0,1:T(8,128)} %collective-permute-done.13, f32[128,576]{0,1:T(8,128)} %collective-permute-done.12, f32[128,576]{0,1:T(8,128)} %collective-permute-done.11, f32[128,576]{0,1:T(8,128)} %collective-permute-done.10, f32[128,576]{0,1:T(8,128)} %collective-permute-done.9, ...), kind=kLoop, calls=%fused_computation.71 | loop fusion | flops 663552 | bytes 3391488 | tf_op jit(solution)/shard_map/convert_element_type | solution.py:110
  (57 shorter events, 10.0 us)
Async XLA Ops:
  0.6 66.3 %copy-start = (bf16[512,1024]{1,0:T(8,128)(2,1)S(1)}, bf16[512,1024]{1,0:T(8,128)(2,1)}, u32[]{:S(2)}) copy-start(bf16[512,1024]{1,0:T(8,128)(2,1)} %param.8) | copy-start | bytes 3145732
  0.6 34.7 %copy-start.9 = (bf16[128,576]{0,1:T(8,128)(2,1)S(1)}, bf16[128,576]{0,1:T(8,128)(2,1)}, u32[]{:S(2)}) copy-start(bf16[128,576]{0,1:T(8,128)(2,1)} %param.7) | copy-start | bytes 442372
  0.7 34.7 %collective-permute-start = (bf16[128,576]{0,1:T(8,128)(2,1)}, bf16[128,576]{0,1:T(8,128)(2,1)}, u32[]{:S(2)}, u32[]{:S(2)}) collective-permute-start(bf16[128,576]{0,1:T(8,128)(2,1)} %param.7), channel_id=1, source_target_pairs={{0,8},{8,16},{16,24},{24,32},{32,40},{40,48},{48,56},{56,64},{64,7... | collective-permute-start | bytes 442376 | tf_op jit(solution)/shard_map/ppermute | solution.py:16
  5.2 36.9 %collective-permute-start.1 = (bf16[128,576]{0,1:T(8,128)(2,1)}, bf16[128,576]{0,1:T(8,128)(2,1)S(1)}, u32[]{:S(2)}, u32[]{:S(2)}) collective-permute-start(bf16[128,576]{0,1:T(8,128)(2,1)} %param.7), channel_id=1, source_target_pairs={{0,16},{8,24},{16,32},{24,40},{32,48},{40,56},{48,64},{56,72},{64,... | collective-permute-start | bytes 442376 | tf_op jit(solution)/shard_map/ppermute | solution.py:16
  9.4 34.0 %collective-permute-start.2 = (bf16[128,576]{0,1:T(8,128)(2,1)}, bf16[128,576]{0,1:T(8,128)(2,1)S(1)}, u32[]{:S(2)}, u32[]{:S(2)}) collective-permute-start(bf16[128,576]{0,1:T(8,128)(2,1)} %param.7), channel_id=1, source_target_pairs={{0,32},{8,40},{16,48},{24,56},{32,64},{40,72},{48,80},{56,88},{64,... | collective-permute-start | bytes 442376 | tf_op jit(solution)/shard_map/ppermute | solution.py:16
  15.1 28.4 %collective-permute-start.3 = (bf16[128,576]{0,1:T(8,128)(2,1)}, bf16[128,576]{0,1:T(8,128)(2,1)S(1)}, u32[]{:S(2)}, u32[]{:S(2)}) collective-permute-start(bf16[128,576]{0,1:T(8,128)(2,1)} %param.7), channel_id=1, source_target_pairs={{0,64},{8,72},{16,80},{24,88},{32,96},{40,104},{48,112},{56,120},{... | collective-permute-start | bytes 442376 | tf_op jit(solution)/shard_map/ppermute | solution.py:16
  18.2 25.3 %collective-permute-start.4 = (bf16[128,576]{0,1:T(8,128)(2,1)}, bf16[128,576]{0,1:T(8,128)(2,1)S(1)}, u32[]{:S(2)}, u32[]{:S(2)}) collective-permute-start(bf16[128,576]{0,1:T(8,128)(2,1)} %param.7), channel_id=1, source_target_pairs={{0,128},{8,136},{16,144},{24,152},{32,160},{40,168},{48,176},{56,1... | collective-permute-start | bytes 442376 | tf_op jit(solution)/shard_map/ppermute | solution.py:16
  35.3 27.4 %collective-permute-start.5 = (bf16[128,576]{0,1:T(8,128)(2,1)S(1)}, bf16[128,576]{0,1:T(8,128)(2,1)S(1)}, u32[]{:S(2)}, u32[]{:S(2)}) collective-permute-start(bf16[128,576]{0,1:T(8,128)(2,1)S(1)} %copy-done.9), channel_id=1, source_target_pairs={{0,256},{8,264},{16,272},{24,280},{32,288},{40,296},{48,304},{56,3... | collective-permute-start | bytes 442376 | tf_op jit(solution)/shard_map/ppermute | solution.py:16
  42.1 20.6 %collective-permute-start.6 = (bf16[128,576]{0,1:T(8,128)(2,1)S(1)}, bf16[128,576]{0,1:T(8,128)(2,1)S(1)}, u32[]{:S(2)}, u32[]{:S(2)}) collective-permute-start(bf16[128,576]{0,1:T(8,128)(2,1)S(1)} %copy-done.9), channel_id=1, source_target_pairs={{0,512},{8,520},{16,528},{24,536},{32,544},{40,552},{48,560},{56,5... | collective-permute-start | bytes 442376 | tf_op jit(solution)/shard_map/ppermute | solution.py:16
  63.4 2.2 %copy-start.2 = (bf16[4,128,576]{1,2,0:T(8,128)(2,1)}, bf16[4,128,576]{1,2,0:T(8,128)(2,1)S(1)}, u32[]{:S(2)}) copy-start(bf16[4,128,576]{1,2,0:T(8,128)(2,1)S(1)} %gather_fusion) | copy-start | bytes 1769476
  68.9 2.3 %copy-start.1 = (bf16[4,128,8,128]{1,3,0,2:T(8,128)(2,1)}, bf16[4,128,8,128]{1,3,0,2:T(8,128)(2,1)S(1)}, u32[]{:S(2)}) copy-start(bf16[4,128,8,128]{1,3,0,2:T(8,128)(2,1)S(1)} %copy.34) | copy-start | bytes 3145732
  68.9 0.9 copy-start.6
  71.2 1.2 copy-start.4
  72.4 1.4 copy-start.7
  77.8 1.5 copy-start.5
  81.0 1.6 copy-start.3
  86.4 8.3 %copy-start.8 = (bf16[8,128,128]{2,1,0:T(8,128)(2,1)S(1)}, bf16[8,128,128]{2,1,0:T(8,128)(2,1)}, u32[]{:S(2)}) copy-start(bf16[8,128,128]{2,1,0:T(8,128)(2,1)} %fusion.12) | copy-start | bytes 786436
  90.2 19.9 %collective-permute-start.13 = (f32[128,576]{0,1:T(8,128)}, f32[128,576]{0,1:T(8,128)}, u32[]{:S(2)}, u32[]{:S(2)}) collective-permute-start(f32[128,576]{0,1:T(8,128)} %bitcast.66), channel_id=1, source_target_pairs={{512,0},{520,8},{528,16},{536,24},{544,32},{552,40},{560,48},{568,... | collective-permute-start | bytes 884744 | tf_op jit(solution)/shard_map/ppermute | solution.py:16
  91.5 45.1 %collective-permute-start.12 = (f32[128,576]{0,1:T(8,128)}, f32[128,576]{0,1:T(8,128)}, u32[]{:S(2)}, u32[]{:S(2)}) collective-permute-start(f32[128,576]{0,1:T(8,128)} %bitcast.64), channel_id=1, source_target_pairs={{256,0},{264,8},{272,16},{280,24},{288,32},{296,40},{304,48},{312,... | collective-permute-start | bytes 884744 | tf_op jit(solution)/shard_map/ppermute | solution.py:16
  95.6 58.0 %collective-permute-start.11 = (f32[128,576]{0,1:T(8,128)}, f32[128,576]{0,1:T(8,128)}, u32[]{:S(2)}, u32[]{:S(2)}) collective-permute-start(f32[128,576]{0,1:T(8,128)} %bitcast.226), channel_id=1, source_target_pairs={{128,0},{136,8},{144,16},{152,24},{160,32},{168,40},{176,48},{184,... | collective-permute-start | bytes 884744 | tf_op jit(solution)/shard_map/ppermute | solution.py:16
  98.1 62.4 %collective-permute-start.10 = (f32[128,576]{0,1:T(8,128)}, f32[128,576]{0,1:T(8,128)}, u32[]{:S(2)}, u32[]{:S(2)}) collective-permute-start(f32[128,576]{0,1:T(8,128)} %bitcast.225), channel_id=1, source_target_pairs={{64,0},{72,8},{80,16},{88,24},{96,32},{104,40},{112,48},{120,56},{... | collective-permute-start | bytes 884744 | tf_op jit(solution)/shard_map/ppermute | solution.py:16
  103.7 75.0 %collective-permute-start.9 = (f32[128,576]{0,1:T(8,128)}, f32[128,576]{0,1:T(8,128)}, u32[]{:S(2)}, u32[]{:S(2)}) collective-permute-start(f32[128,576]{0,1:T(8,128)} %bitcast.224), channel_id=1, source_target_pairs={{32,0},{40,8},{48,16},{56,24},{64,32},{72,40},{80,48},{88,56},{96,... | collective-permute-start | bytes 884744 | tf_op jit(solution)/shard_map/ppermute | solution.py:16
  110.1 76.8 %collective-permute-start.8 = (f32[128,576]{0,1:T(8,128)}, f32[128,576]{0,1:T(8,128)}, u32[]{:S(2)}, u32[]{:S(2)}) collective-permute-start(f32[128,576]{0,1:T(8,128)} %bitcast.56), channel_id=1, source_target_pairs={{16,0},{24,8},{32,16},{40,24},{48,32},{56,40},{64,48},{72,56},{80,... | collective-permute-start | bytes 884744 | tf_op jit(solution)/shard_map/ppermute | solution.py:16
  136.7 54.7 %collective-permute-start.7 = (f32[128,576]{0,1:T(8,128)}, f32[128,576]{0,1:T(8,128)}, u32[]{:S(2)}, u32[]{:S(2)}) collective-permute-start(f32[128,576]{0,1:T(8,128)} %bitcast.54), channel_id=1, source_target_pairs={{8,0},{16,8},{24,16},{32,24},{40,32},{48,40},{56,48},{64,56},{72,6... | collective-permute-start | bytes 884744 | tf_op jit(solution)/shard_map/ppermute | solution.py:16
where the time goes:
time: 195 us; the launch traced here: 194 us
  waiting for transfers between devices  92.8 us (48%)
  starting transfers between devices  50.2 us (26%)
  matrix products  22.7 us (12%)
  local copies, waits for them, and re-layouts  16.8 us (9%)
  between operations  6.21 us (3%)
  other arithmetic  4.98 us (3%)
    ppermute x14, waiting for transfers between devices, passed_along(): return lax.ppermute(shard, axis, pairs)  92.8 us
    ppermute x14, starting transfers between devices, passed_along(): return lax.ppermute(shard, axis, pairs)  50.2 us
    unnamed x33, local copies, waits for them, and re-layouts  9.54 us
    dot_general x7, matrix products, on_device(): piece = jnp.tensordot(weight, share, axes=1)  8.83 us
  transfers between devices with their start and end apart: 14, of which 8 were waited for; matrix products, arithmetic and copies ran while one was open for 8% of the time, Pallas kernels for 0%

commit v1 on v0

v1 whole, which is shorter than its diff:
```python
import jax
import jax.numpy as jnp
from jax import lax
from jax.experimental import pallas as pl
from jax.experimental.pallas import tpu as pltpu
from jax.sharding import PartitionSpec as P

HEADS = 8
NOPE = 128
ROPE = 64
LATENT = 512
SLOTS = 4
TOK = 128
NY = 8
NZ = 16
LEVELS = 8
WIRE = 576
PART_A = (384, 192)
PART_B = ((0, 192), (192, 192))
PARTS = (PART_A,) + PART_B
MESH = pl.DeviceIdType.MESH
F32 = jnp.float32
BF16 = jnp.bfloat16


class Move:
    def __init__(self, src, dst, dz, dy, valid):
        self.src, self.dst, self.dz, self.dy, self.valid = src, dst, dz, dy, valid


class Exchange:
    def __init__(self, moves, send_sem, recv_sem):
        self.moves, self.send_sem, self.recv_sem = moves, send_sem, recv_sem
        self.order = {name: i for i, name in enumerate(moves)}
        position = lax.axis_index("ctx")
        self.z = lax.div(position, NY)
        self.y = lax.rem(position, NY)

    def at(self, dz, dy):
        return lax.rem(self.z + dz + NZ, NZ), lax.rem(self.y + dy + NY, NY)

    def index(self, dz, dy):
        z, y = self.at(dz, dy)
        return z * NY + y

    def sends(self, name):
        return self.moves[name].valid(self.z, self.y)

    def receives(self, name):
        move = self.moves[name]
        return move.valid(*self.at(-move.dz, -move.dy))

    def barrier(self):
        barrier = pltpu.get_barrier_semaphore()
        groups = {}
        for name, move in self.moves.items():
            groups.setdefault((move.dz, move.dy), []).append(name)
        waits = jnp.int32(0)
        for (dz, dy), names in groups.items():
            out, into = self.sends(names[0]), self.receives(names[0])
            for name in names[1:]:
                out, into = out | self.sends(name), into | self.receives(name)
            waits = waits + out.astype(jnp.int32)

            @pl.when(into)
            def _():
                pl.semaphore_signal(
                    barrier, inc=1, device_id={"ctx": self.index(-dz, -dy)}, device_id_type=MESH
                )

        pl.semaphore_wait(barrier, waits)

    def copy(self, name):
        move, i = self.moves[name], self.order[name]
        return pltpu.make_async_remote_copy(
            src_ref=move.src,
            dst_ref=move.dst,
            send_sem=self.send_sem.at[i],
            recv_sem=self.recv_sem.at[i],
            device_id={"ctx": self.index(move.dz, move.dy)},
            device_id_type=MESH,
        )

    def start(self, name):
        @pl.when(self.sends(name))
        def _():
            self.copy(name).start()

    def wait(self, name):
        @pl.when(self.receives(name))
        def _():
            self.copy(name).wait_recv()

    def finish(self):
        for name in self.moves:

            @pl.when(self.sends(name))
            def _():
                self.copy(name).wait_send()


def rows(ref, part, lead=None):
    window = pl.ds(part[0], part[1])
    return ref.at[window] if lead is None else ref.at[lead, window]


def outward_moves(cand, passed):
    moves = {}
    for i, part in enumerate(PARTS):
        own, l4, l5 = rows(cand, part, 0), rows(cand, part, 4), rows(cand, part, 5)
        l6, l7 = rows(cand, part, 6), rows(cand, part, 7)
        moves["one", i] = Move(own, l4, 1, 0, lambda z, y: z < 15)
        moves["two", i] = Move(l4, l5, 1, 0, lambda z, y: (z >= 1) & (z < 15))
        moves["four", i] = Move(l5, l6, 2, 0, lambda z, y: (z >= 2) & (z < 14))
        if i == 0:
            moves["eight", i] = Move(l6, l7, 4, 0, lambda z, y: (z >= 4) & (z < 12))
        else:
            via = passed.at[i - 1]
            moves["back", i] = Move(own, via, -4, 0, lambda z, y: z < 8)
            moves["on", i] = Move(via, l7, -4, 0, lambda z, y: (z < 4) | (z >= 12))
    for k in range(3):
        by = 2**k
        moves["near", k] = Move(cand.at[0], cand.at[k + 1], 0, by, lambda z, y, by=by: y + by < NY)
        moves["cross", k] = Move(
            cand.at[4], cand.at[k + 1], 0, by, lambda z, y, by=by: (y + by >= NY) & (z >= 1)
        )
    return moves


def pack_rope(rope):
    return jnp.concatenate([rope[:64], rope[64:]], axis=1)


def gather_kernel(lat_ref, cand, passed, send_sem, recv_sem):
    for c in range(4):
        cand[0, c * 128 : (c + 1) * 128, :] = lat_ref[:, c * 128 : (c + 1) * 128]
    cand[0, 512:576, :] = pack_rope(lat_ref[:, 512:576].astype(F32)).astype(BF16)
    ex = Exchange(outward_moves(cand, passed), send_sem, recv_sem)
    ex.barrier()
    for i in (1, 2):
        ex.start(("back", i))
    for i in range(3):
        ex.start(("one", i))
    for k in (2, 1, 0):
        ex.start(("near", k))
    for i in range(3):
        ex.wait(("one", i))
        ex.start(("two", i))
    for k in (2, 1, 0):
        ex.start(("cross", k))
    for i in (1, 2):
        ex.wait(("back", i))
        ex.start(("on", i))
    for i in range(3):
        ex.wait(("two", i))
        ex.start(("four", i))
    for i in range(3):
        ex.wait(("four", i))
        if i == 0:
            ex.start(("eight", 0))
    for k in range(3):
        ex.wait(("near", k))
        ex.wait(("cross", k))
    ex.wait(("eight", 0))
    for i in (1, 2):
        ex.wait(("on", i))
    ex.finish()


def gather(latents):
    vmem = pl.BlockSpec(memory_space=pltpu.VMEM)
    count = 3 * 3 + 1 + 4 + 6
    return pl.pallas_call(
        gather_kernel,
        out_shape=jax.ShapeDtypeStruct((LEVELS, WIRE, 128), BF16),
        in_specs=[vmem],
        out_specs=vmem,
        scratch_shapes=[
            pltpu.VMEM((2, 192, 128), BF16),
            pltpu.SemaphoreType.DMA((count,)),
            pltpu.SemaphoreType.DMA((count,)),
        ],
        compiler_params=pltpu.CompilerParams(
            collective_id=0, has_side_effects=True, vmem_limit_bytes=16 * 2**20
        ),
        name="latents_out",
    )(latents)


def attend_kernel(
    mask_ref, q_ref, cand, ku_ref, vu_ref, og_ref, att_ref, gq_ref, pieces, own_ref,
    qa, keys, values, rope, pk, pv, share,
):
    position = lax.axis_index("ctx")
    rank = jnp.int32(1)
    level_of = [jnp.int32(0) for _ in range(SLOTS)]
    slot_of = [jnp.int32(0)]
    for level in range(1, LEVELS):
        source = position - 2 ** (level - 1)
        linked = (source >= 0) & (mask_ref[0, jnp.maximum(source, 0)] == 1) & (rank < SLOTS)
        for j in range(1, SLOTS):
            level_of[j] = jnp.where(linked & (rank == j), level, level_of[j])
        slot_of.append(jnp.where(linked, rank, SLOTS))
        rank = rank + linked.astype(jnp.int32)

    scale = (NOPE + ROPE) ** -0.5
    lane = lax.broadcasted_iota(jnp.int32, (64, 128), 1)
    zeros = jnp.zeros((TOK, 64), BF16)
    for h in range(HEADS):
        base = h * (NOPE + ROPE)
        qa[:, h * 256 : (h + 1) * 256] = jnp.concatenate(
            [q_ref[:, base : base + 192].astype(F32), zeros.astype(F32)], axis=1
        ).astype(BF16)
    for j in range(SLOTS):
        block = cand[level_of[j]]
        plain = jnp.concatenate([block[c * 128 : (c + 1) * 128] for c in range(4)], axis=1)
        keys[j * TOK : (j + 1) * TOK, :] = jnp.dot(
            plain, ku_ref[...], preferred_element_type=F32
        ).astype(BF16)
        values[j * TOK : (j + 1) * TOK, :] = jnp.dot(
            plain, vu_ref[...], preferred_element_type=F32
        ).astype(BF16)
        packed = block[512:576].astype(F32)
        rope[j * TOK : j * TOK + 64, :] = jnp.where(lane < 64, packed, 0.0).astype(BF16)
        rope[j * TOK + 64 : (j + 1) * TOK, :] = jnp.where(
            lane < 64, pltpu.roll(packed, 64, 1), 0.0
        ).astype(BF16)
    t = lax.broadcasted_iota(jnp.int32, (TOK, SLOTS * TOK), 0)
    s = lax.broadcasted_iota(jnp.int32, (TOK, SLOTS * TOK), 1)
    edge = jnp.where(
        s < TOK, t, jnp.where(s < rank * TOK, SLOTS * TOK, -1)
    )
    allowed = edge >= s
    nt = (((1,), (1,)), ((), ()))
    tn = (((0,), (0,)), ((), ()))
    rope_sum = jnp.zeros((SLOTS * TOK, 128), F32)
    for h in range(HEADS):
        cols = slice(h * 128, (h + 1) * 128)
        q_h = qa[:, h * 256 : (h + 1) * 256]
        k_h = jnp.concatenate([keys[:, cols], rope[...]], axis=1)
        v_h = values[:, cols]
        g_h = og_ref[:, cols]
        scores = lax.dot_general(q_h, k_h, nt, preferred_element_type=F32)
        scores = jnp.where(allowed, scores, -jnp.inf)
        peak = jnp.max(scores, axis=1, keepdims=True)
        powers = jnp.exp((scores - peak) * scale)
        probs = powers * (1.0 / jnp.sum(powers, axis=1, keepdims=True))
        probs_bf = probs.astype(BF16)
        att_ref[:, cols] = jnp.dot(probs_bf, v_h, preferred_element_type=F32).astype(BF16)
        dprobs = lax.dot_general(g_h, v_h, nt, preferred_element_type=F32)
        delta = jnp.sum(probs * dprobs, axis=1, keepdims=True)
        dscores = (probs * (dprobs - delta) * scale).astype(BF16)
        dq = jnp.dot(dscores, k_h, preferred_element_type=F32)
        base = h * (NOPE + ROPE)
        gq_ref[:, base : base + 192] = dq[:, :192].astype(BF16)
        dk = lax.dot_general(dscores, q_h, tn, preferred_element_type=F32)
        pk[:, cols] = dk[:, :128].astype(BF16)
        rope_sum = rope_sum + dk[:, 128:]
        pv[:, cols] = lax.dot_general(
            probs_bf, g_h, tn, preferred_element_type=F32
        ).astype(BF16)
    share[SLOTS] = jnp.zeros((WIRE, 128), BF16)
    for j in range(SLOTS):
        part = slice(j * TOK, (j + 1) * TOK)
        grad = lax.dot_general(pk[part], ku_ref[...], nt, preferred_element_type=F32)
        grad = grad + lax.dot_general(pv[part], vu_ref[...], nt, preferred_element_type=F32)
        turned = rope_sum[j * TOK : j * TOK + 64] + pltpu.roll(
            rope_sum[j * TOK + 64 : (j + 1) * TOK], 64, 1
        )
        for c in range(4):
            block = grad[:, c * 128 : (c + 1) * 128]
            if j == 0:
                own_ref[c * 128 : (c + 1) * 128, :] = block
            else:
                share[j, c * 128 : (c + 1) * 128, :] = block.astype(BF16)
        if j == 0:
            own_ref[512:576, :] = turned
        else:
            share[j, 512:576, :] = turned.astype(BF16)
    for level in range(1, LEVELS):
        pieces[level - 1] = share[slot_of[level]]


def attend(link_mask, queries, cand, key_up, value_up, out_grad):
    vmem = pl.BlockSpec(memory_space=pltpu.VMEM)
    width = HEADS * NOPE
    return pl.pallas_call(
        attend_kernel,
        out_shape=(
            jax.ShapeDtypeStruct((TOK, width), BF16),
            jax.ShapeDtypeStruct((TOK, HEADS * (NOPE + ROPE)), BF16),
            jax.ShapeDtypeStruct((LEVELS - 1, WIRE, 128), BF16),
            jax.ShapeDtypeStruct((WIRE, 128), F32),
        ),
        in_specs=[pl.BlockSpec(memory_space=pltpu.SMEM)] + [vmem] * 5,
        out_specs=(vmem,) * 4,
        scratch_shapes=[
            pltpu.VMEM((TOK, HEADS * 256), BF16),
            pltpu.VMEM((SLOTS * TOK, width), BF16),
            pltpu.VMEM((SLOTS * TOK, width), BF16),
            pltpu.VMEM((SLOTS * TOK, 128), BF16),
            pltpu.VMEM((SLOTS * TOK, width), BF16),
            pltpu.VMEM((SLOTS * TOK, width), BF16),
            pltpu.VMEM((SLOTS + 1, WIRE, 128), BF16),
        ],
        compiler_params=pltpu.CompilerParams(vmem_limit_bytes=48 * 2**20),
        name="attend",
    )(link_mask, queries, cand, key_up, value_up, out_grad)


def homeward_moves(pieces, r8, r4, r2, r1, t4, t2, t1, passed, far, near):
    moves = {}
    for i, part in enumerate(PARTS):
        p7 = rows(pieces, part, 6)
        if i == 0:
            moves["eight", i] = Move(p7, r8, -4, 0, lambda z, y: z >= 8)
            src = rows(t4, part)
        else:
            via, last = passed.at[i - 1], rows(far, part)
            moves["back", i] = Move(p7, via, 4, 0, lambda z, y: z >= 8)
            moves["on", i] = Move(via, last, 4, 0, lambda z, y: (z < 4) | (z >= 12))
            src = rows(pieces, part, 5)
        moves["four", i] = Move(src, rows(r4, part), -2, 0, lambda z, y: z >= 4)
        moves["two", i] = Move(rows(t2, part), rows(r2, part), -1, 0, lambda z, y: z >= 2)
        moves["one", i] = Move(rows(t1, part), rows(r1, part), -1, 0, lambda z, y: z >= 1)
    for k in range(3):
        by = 2**k
        moves["near", k] = Move(
            pieces.at[k], near.at[k], 0, -by, lambda z, y, by=by: (y >= by) | (z >= 1)
        )
    return moves


def home_kernel(
    pieces, own_ref, out_ref, r8, r4, r2, r1, t4, t2, t1, passed, far, near, send_sem, recv_sem
):
    ex = Exchange(
        homeward_moves(pieces, r8, r4, r2, r1, t4, t2, t1, passed, far, near), send_sem, recv_sem
    )
    z, y = ex.z, ex.y

    def piece(level, part):
        return pieces[level - 1, part[0] : part[0] + part[1], :].astype(F32)

    def got(ref, part, valid):
        return jnp.where(valid, ref[part[0] : part[0] + part[1], :].astype(F32), 0.0)

    ex.barrier()
    for i in (1, 2):
        ex.start(("back", i))
    ex.start(("eight", 0))
    for i in (1, 2):
        ex.start(("four", i))
    for k in (2, 1, 0):
        ex.start(("near", k))
    ex.wait(("eight", 0))
    a0, a1 = PART_A[0], PART_A[0] + PART_A[1]
    t4[a0:a1, :] = (piece(6, PART_A) + jnp.where(z <= 11, r8[...].astype(F32), 0.0)).astype(BF16)
    ex.start(("four", 0))
    for i in (1, 2):
        ex.wait(("back", i))
        ex.start(("on", i))
    for i in (1, 2, 0):
        part = PARTS[i]
        ex.wait(("four", i))
        t2[part[0] : part[0] + part[1], :] = (
            piece(5, part) + got(r4, part, z <= 13)
        ).astype(BF16)
        ex.start(("two", i))
    for k in range(3):
        ex.wait(("near", k))
    for i in (1, 2, 0):
        part = PARTS[i]
        ex.wait(("two", i))
        total = piece(4, part) + got(r2, part, z <= 14)
        for k in range(3):
            total = total + got(near.at[k], part, y + 2**k >= NY)
        t1[part[0] : part[0] + part[1], :] = total.astype(BF16)
        ex.start(("one", i))
    for i in (1, 2):
        ex.wait(("on", i))
    sums = {}
    for i in (1, 2, 0):
        part = PARTS[i]
        ex.wait(("one", i))
        total = own_ref[part[0] : part[0] + part[1], :] + got(r1, part, z <= 14)
        for k in range(3):
            total = total + got(near.at[k], part, y + 2**k < NY)
        if i > 0:
            total = total + got(far, part, z < 8)
        sums[i] = total
    whole = jnp.concatenate([sums[1], sums[2], sums[0]], axis=0)
    for c in range(4):
        out_ref[:, c * 128 : (c + 1) * 128] = whole[c * 128 : (c + 1) * 128].astype(BF16)
    turned = whole[512:576]
    out_ref[:64, 512:576] = turned[:, :64].astype(BF16)
    out_ref[64:, 512:576] = pltpu.roll(turned, 64, 1)[:, :64].astype(BF16)
    ex.finish()


def home(pieces, own):
    vmem = pl.BlockSpec(memory_space=pltpu.VMEM)
    block = pltpu.VMEM((WIRE, 128), BF16)
    count = 1 + 4 + 9 + 3
    return pl.pallas_call(
        home_kernel,
        out_shape=jax.ShapeDtypeStruct((TOK, LATENT + ROPE), BF16),
        in_specs=[vmem, vmem],
        out_specs=vmem,
        scratch_shapes=[
            pltpu.VMEM((192, 128), BF16),
            block, block, block, block, block, block,
            pltpu.VMEM((2, 192, 128), BF16),
            block,
            pltpu.VMEM((3, WIRE, 128), BF16),
            pltpu.SemaphoreType.DMA((count,)),
            pltpu.SemaphoreType.DMA((count,)),
        ],
        compiler_params=pltpu.CompilerParams(
            collective_id=1, has_side_effects=True, vmem_limit_bytes=16 * 2**20
        ),
        name="gradients_home",
    )(pieces, own)


def on_device(queries, latents, key_up, value_up, link_mask, out_grad):
    cand = gather(latents)
    attention, grad_queries, pieces, own = attend(
        link_mask, queries, cand, key_up, value_up, out_grad
    )
    return attention, grad_queries, home(pieces, own)


def solution(mesh):
    split = P(("dp", "ctx"), None)
    return jax.shard_map(
        on_device,
        mesh=mesh,
        in_specs=(split, split, P(), P(), split, split),
        out_specs=(split, split, split),
        check_vma=False,
    )
```

time: 195 us -> 84.8 us (0.43)
  the two profiles are of different devices: /device:TPU:507 before, /device:TPU:6 now
where the time goes in v1:
time: 84.8 us; the launch traced here: 84.5 us
  Pallas kernels  79.7 us (94%)
  local copies, waits for them, and re-layouts  4.14 us (5%)
    pallas_call x1, Pallas kernels, gather(): pl.pallas_call(gather_kernel, out_shape=jax.ShapeDtypeStruct((LEVELS, WIR...  34.7 us
    pallas_call x1, Pallas kernels, home(): pl.pallas_call(home_kernel, out_shape=jax.ShapeDtypeStruct((TOK, LATENT +...  34.5 us
    pallas_call x1, Pallas kernels, attend(): pl.pallas_call(attend_kernel, out_shape=(jax.ShapeDtypeStruct((TOK, width...  10.5 us
    unnamed x12, local copies, waits for them, and re-layouts  4.14 us

profile of v1, /device:TPU:6, one launch (start us, length us, event | category | flops | bytes accessed | tf_op | source)
XLA Modules:
  0.0 84.5 jit_solution(5606626930773096125)
XLA Ops:
  0.6 0.0 copy-start.4
  0.6 0.0 copy-start
  0.7 0.0 copy-start.2
  0.7 1.2 %copy.9.lat_ref = bf16[128,576]{1,0:T(8,128)(2,1)S(1)} copy(bf16[128,576]{0,1:T(8,128)(2,1)} %param.7) | data formatting | bytes 294912 | tf_op args[1]
  1.8 34.7 %latents_out.1.cand = bf16[8,576,128]{2,1,0:T(8,128)(2,1)S(1)} custom-call(bf16[128,576]{1,0:T(8,128)(2,1)S(1)} %copy.9.lat_ref), custom_call_target="tpu_custom_call" | custom-call | tf_op jit(solution)/shard_map/latents_out/pallas_call | solution.py:173
  36.5 0.0 copy-done.4
  36.5 0.0 copy-done
  36.5 0.0 copy-done.2
  36.5 0.0 copy-start.1
  36.5 1.2 %copy-done.1 = bf16[512,1024]{1,0:T(8,128)(2,1)S(1)} copy-done((bf16[512,1024]{1,0:T(8,128)(2,1)S(1)}, bf16[512,1024]{1,0:T(8,128)(2,1)}, u32[]{:S(2)}) %copy-start.1) | copy-done | bytes 1048600
  37.8 0.0 copy-start.3
  37.8 0.9 %copy-done.3 = bf16[128,1024]{1,0:T(8,128)(2,1)S(1)} copy-done((bf16[128,1024]{1,0:T(8,128)(2,1)S(1)}, bf16[128,1024]{1,0:T(8,128)(2,1)}, u32[]{:S(2)}) %copy-start.3) | copy-done | bytes 262168
  38.7 10.5 %attend.1 = (bf16[128,1024]{1,0:T(8,128)(2,1)}, bf16[128,1536]{1,0:T(8,128)(2,1)}, bf16[7,576,128]{2,1,0:T(8,128)(2,1)S(1)}, f32[576,128]{1,0:T(8,128)S(1)}) custom-call(s32[1,128]{1,0:T(1,128)S(1)} %copy-done.4, bf16[128,1536]{1,0:T(8,128)(2,1)S(1)} %copy-done.2, bf16[8,576,128]{2,1,0:T(8,128)(2,1)S(1)} %latents_out.1.cand, bf16[512,1024]{1,0:T(8,128)(2,1)S(1)} %copy-done, ...), custom_call_target="tpu_custom_call" | custom-call | tf_op jit(solution)/shard_map/attend/pallas_call | solution.py:287
  49.2 34.5 %gradients_home.1 = bf16[128,576]{1,0:T(8,128)(2,1)S(1)} custom-call(bf16[7,576,128]{2,1,0:T(8,128)(2,1)S(1)} %get-tuple-element.9.pieces, f32[576,128]{1,0:T(8,128)S(1)} %get-tuple-element.10.own_ref), custom_call_target="tpu_custom_call" | custom-call | tf_op jit(solution)/shard_map/gradients_home/pallas_call | solution.py:405
  83.8 0.8 copy.10
Async XLA Ops:
  0.6 35.9 %copy-start.4 = (s32[1,128]{1,0:T(1,128)S(1)}, s32[1,128]{1,0:T(1,128)}, u32[]{:S(2)}) copy-start(s32[1,128]{1,0:T(1,128)} %mask_ref.1) | copy-start | bytes 1540
  0.6 35.9 %copy-start = (bf16[512,1024]{1,0:T(8,128)(2,1)S(1)}, bf16[512,1024]{1,0:T(8,128)(2,1)}, u32[]{:S(2)}) copy-start(bf16[512,1024]{1,0:T(8,128)(2,1)} %ku_ref.1) | copy-start | bytes 3145732
  0.7 35.9 %copy-start.2 = (bf16[128,1536]{1,0:T(8,128)(2,1)S(1)}, bf16[128,1536]{1,0:T(8,128)(2,1)}, u32[]{:S(2)}) copy-start(bf16[128,1536]{1,0:T(8,128)(2,1)} %q_ref.1) | copy-start | bytes 1179652
  36.5 1.2 %copy-start.1 = (bf16[512,1024]{1,0:T(8,128)(2,1)S(1)}, bf16[512,1024]{1,0:T(8,128)(2,1)}, u32[]{:S(2)}) copy-start(bf16[512,1024]{1,0:T(8,128)(2,1)} %vu_ref.1) | copy-start | bytes 3145732
  37.8 0.9 %copy-start.3 = (bf16[128,1024]{1,0:T(8,128)(2,1)S(1)}, bf16[128,1024]{1,0:T(8,128)(2,1)}, u32[]{:S(2)}) copy-start(bf16[128,1024]{1,0:T(8,128)(2,1)} %og_ref.1) | copy-start | bytes 786436

commit v2 on v1

v2 whole, which is shorter than its diff:
```python
import jax
import jax.numpy as jnp
from jax import lax
from jax.experimental import pallas as pl
from jax.experimental.pallas import tpu as pltpu
from jax.sharding import PartitionSpec as P

HEADS = 8
NOPE = 128
ROPE = 64
LATENT = 512
SLOTS = 4
TOK = 128
NY = 8
NZ = 16
LEVELS = 8
WIDTH = HEADS * NOPE
WIRE = LATENT + ROPE
PART_A = (384, 192)
PART_B = ((0, 192), (192, 192))
PARTS = (PART_A,) + PART_B
MESH = pl.DeviceIdType.MESH
F32 = jnp.float32
BF16 = jnp.bfloat16


class Move:
    def __init__(self, src, dst, dz, dy, valid):
        self.src, self.dst, self.dz, self.dy, self.valid = src, dst, dz, dy, valid


class Exchange:
    def __init__(self, moves, send_sem, recv_sem):
        self.moves, self.send_sem, self.recv_sem = moves, send_sem, recv_sem
        self.order = {name: i for i, name in enumerate(moves)}
        position = lax.axis_index("ctx")
        self.z = lax.div(position, NY)
        self.y = lax.rem(position, NY)

    def at(self, dz, dy):
        return lax.rem(self.z + dz + NZ, NZ), lax.rem(self.y + dy + NY, NY)

    def index(self, dz, dy):
        z, y = self.at(dz, dy)
        return z * NY + y

    def sends(self, name):
        return self.moves[name].valid(self.z, self.y)

    def receives(self, name):
        move = self.moves[name]
        return move.valid(*self.at(-move.dz, -move.dy))

    def barrier(self):
        barrier = pltpu.get_barrier_semaphore()
        groups = {}
        for name, move in self.moves.items():
            groups.setdefault((move.dz, move.dy), []).append(name)
        waits = jnp.int32(0)
        for (dz, dy), names in groups.items():
            out, into = self.sends(names[0]), self.receives(names[0])
            for name in names[1:]:
                out, into = out | self.sends(name), into | self.receives(name)
            waits = waits + out.astype(jnp.int32)

            @pl.when(into)
            def _():
                pl.semaphore_signal(
                    barrier, inc=1, device_id={"ctx": self.index(-dz, -dy)}, device_id_type=MESH
                )

        pl.semaphore_wait(barrier, waits)

    def copy(self, name):
        move, i = self.moves[name], self.order[name]
        return pltpu.make_async_remote_copy(
            src_ref=move.src,
            dst_ref=move.dst,
            send_sem=self.send_sem.at[i],
            recv_sem=self.recv_sem.at[i],
            device_id={"ctx": self.index(move.dz, move.dy)},
            device_id_type=MESH,
        )

    def start(self, name):
        @pl.when(self.sends(name))
        def _():
            self.copy(name).start()

    def wait(self, name):
        @pl.when(self.receives(name))
        def _():
            self.copy(name).wait_recv()

    def finish(self):
        for name in self.moves:

            @pl.when(self.sends(name))
            def _():
                self.copy(name).wait_send()


def rows(ref, part, lead=None):
    window = pl.ds(part[0], part[1])
    return ref.at[window] if lead is None else ref.at[lead, window]


def outward_moves(own, cand, passed):
    moves = {}
    for i, part in enumerate(PARTS):
        mine, l4, l5 = rows(own, part), rows(cand, part, 4), rows(cand, part, 5)
        l6, l7 = rows(cand, part, 6), rows(cand, part, 7)
        moves["out one", i] = Move(mine, l4, 1, 0, lambda z, y: z < 15)
        moves["out two", i] = Move(l4, l5, 1, 0, lambda z, y: (z >= 1) & (z < 15))
        moves["out four", i] = Move(l5, l6, 2, 0, lambda z, y: (z >= 2) & (z < 14))
        if i == 0:
            moves["out eight", i] = Move(l6, l7, 4, 0, lambda z, y: (z >= 4) & (z < 12))
        else:
            via = passed.at[i - 1]
            moves["out back", i] = Move(mine, via, -4, 0, lambda z, y: z < 8)
            moves["out on", i] = Move(via, l7, -4, 0, lambda z, y: (z < 4) | (z >= 12))
    for k in range(3):
        by = 2**k
        moves["out near", k] = Move(own, cand.at[k + 1], 0, by, lambda z, y, by=by: y + by < NY)
        moves["out cross", k] = Move(
            cand.at[4], cand.at[k + 1], 0, by, lambda z, y, by=by: (y + by >= NY) & (z >= 1)
        )
    return moves


def homeward_moves(pieces, r8, r4, r2, r1, t4, t2, t1, passed, far, near):
    moves = {}
    for i, part in enumerate(PARTS):
        p7 = rows(pieces, part, 6)
        if i == 0:
            moves["eight", i] = Move(p7, r8, -4, 0, lambda z, y: z >= 8)
            src = rows(t4, part)
        else:
            via, last = passed.at[i - 1], rows(far, part)
            moves["back", i] = Move(p7, via, 4, 0, lambda z, y: z >= 8)
            moves["on", i] = Move(via, last, 4, 0, lambda z, y: (z < 4) | (z >= 12))
            src = rows(pieces, part, 5)
        moves["four", i] = Move(src, rows(r4, part), -2, 0, lambda z, y: z >= 4)
        moves["two", i] = Move(rows(t2, part), rows(r2, part), -1, 0, lambda z, y: z >= 2)
        moves["one", i] = Move(rows(t1, part), rows(r1, part), -1, 0, lambda z, y: z >= 1)
    for k in range(3):
        by = 2**k
        moves["near", k] = Move(
            pieces.at[k], near.at[k], 0, -by, lambda z, y, by=by: (y >= by) | (z >= 1)
        )
    return moves


MOVES = 20 + 17
NT = (((1,), (1,)), ((), ()))
TN = (((0,), (0,)), ((), ()))


def dot(a, b, dims=(((1,), (0,)), ((), ()))):
    return lax.dot_general(a, b, dims, preferred_element_type=F32)


def kernel(
    mask_ref, q_hbm, lat_hbm, ku_hbm, vu_hbm, og_hbm, att_ref, gq_ref, gl_ref,
    q_ref, ku_ref, vu_ref, og_ref, cand, out_passed,
    qa, keys, values, rope, near_scores, near_dprobs, probs, dscores, pk, pv,
    share, pieces, own_grad, r8, r4, r2, r1, t4, t2, t1, passed, far, near,
    local_sem, send_sem, recv_sem,
):
    moves = outward_moves(lat_hbm, cand, out_passed)
    moves.update(homeward_moves(pieces, r8, r4, r2, r1, t4, t2, t1, passed, far, near))
    ex = Exchange(moves, send_sem, recv_sem)
    z, y = ex.z, ex.y
    local = {
        name: pltpu.make_async_copy(src, dst, local_sem.at[i])
        for i, (name, src, dst) in enumerate(
            (
                ("own", lat_hbm, cand.at[0]),
                ("q", q_hbm, q_ref),
                ("ku", ku_hbm, ku_ref),
                ("vu", vu_hbm, vu_ref),
                ("og", og_hbm, og_ref),
            )
        )
    }
    for copy in local.values():
        copy.start()

    position = lax.axis_index("ctx")
    first = (position >= 1) & (mask_ref[0, jnp.maximum(position - 1, 0)] == 1)
    found = jnp.int32(0)
    level_of = [jnp.int32(0), jnp.int32(0)]
    slot_of = {}
    for level in range(2, LEVELS):
        source = position - 2 ** (level - 1)
        linked = (source >= 0) & (mask_ref[0, jnp.maximum(source, 0)] == 1) & (found < 2)
        for j in range(2):
            level_of[j] = jnp.where(linked & (found == j), level, level_of[j])
        slot_of[level] = jnp.where(linked, found, 2)
        found = found + linked.astype(jnp.int32)
    scale = (NOPE + ROPE) ** -0.5
    no = -jnp.inf
    t = lax.broadcasted_iota(jnp.int32, (TOK, 2 * TOK), 0)
    s = lax.broadcasted_iota(jnp.int32, (TOK, 2 * TOK), 1)
    near_allowed = jnp.where(s < TOK, t, jnp.where(first, 2 * TOK, -1)) >= s
    far_bias = jnp.where(lax.broadcasted_iota(jnp.int32, (1, 2 * TOK), 1) < found * TOK, 0.0, no)

    def rope_rows(j, block):
        padded = jnp.concatenate([block, jnp.zeros((64, TOK), BF16)], axis=0)
        rope[j * TOK : (j + 1) * TOK, :] = padded.astype(F32).T.astype(BF16)

    def project(j, blocks):
        part = slice(j * TOK, j * TOK + blocks.shape[1])
        keys[part, :] = dot(blocks, ku_ref[...], TN).astype(BF16)
        values[part, :] = dot(blocks, vu_ref[...], TN).astype(BF16)

    def near_head(h):
        cols = slice(h * 128, (h + 1) * 128)
        k_h = jnp.concatenate([keys[: 2 * TOK, cols], rope[: 2 * TOK, :]], axis=1)
        scores = dot(qa[:, h * 256 : (h + 1) * 256], k_h, NT)
        near_scores[h] = jnp.where(near_allowed, scores, no)
        near_dprobs[h] = dot(og_ref[:, cols], values[: 2 * TOK, cols], NT)

    ex.barrier()
    for i in (1, 2):
        ex.start(("out back", i))
    for i in range(3):
        ex.start(("out one", i))
    for k in (2, 1, 0):
        ex.start(("out near", k))
    local["q"].wait()
    for h in range(HEADS):
        base = h * (NOPE + ROPE)
        qa[:, h * 256 : (h + 1) * 256] = jnp.concatenate(
            [q_ref[:, base : base + 192].astype(F32), jnp.zeros((TOK, 64), F32)], axis=1
        ).astype(BF16)
    for i in range(3):
        ex.wait(("out one", i))
        ex.start(("out two", i))
    for k in (2, 1, 0):
        ex.start(("out cross", k))
    for name in ("own", "ku", "vu", "og"):
        local[name].wait()
    project(0, cand[0, :LATENT])
    rope_rows(0, cand[0, LATENT:])
    for i in (1, 2):
        ex.wait(("out back", i))
        ex.start(("out on", i))
    for i in range(3):
        ex.wait(("out two", i))
        ex.start(("out four", i))
    ex.wait(("out near", 0))
    ex.wait(("out cross", 0))
    project(1, cand[1, :LATENT])
    rope_rows(1, cand[1, LATENT:])
    ex.wait(("out four", 0))
    ex.start(("out eight", 0))
    for h in range(HEADS):
        near_head(h)
    for i in (1, 2):
        ex.wait(("out four", i))
    for k in (1, 2):
        ex.wait(("out near", k))
        ex.wait(("out cross", k))
    ex.wait(("out eight", 0))
    for i in (1, 2):
        ex.wait(("out on", i))

    far_rows = slice(2 * TOK, 4 * TOK)
    two, three = cand[level_of[0]], cand[level_of[1]]
    project(2, jnp.concatenate([two[:LATENT], three[:LATENT]], axis=1))
    rope_rows(2, two[LATENT:])
    rope_rows(3, three[LATENT:])
    rope_sum = jnp.zeros((2 * TOK, 128), F32)
    for h in range(HEADS):
        cols = slice(h * 128, (h + 1) * 128)
        q_h = qa[:, h * 256 : (h + 1) * 256]
        g_h = og_ref[:, cols]
        k_h = jnp.concatenate([keys[far_rows, cols], rope[far_rows, :]], axis=1)
        scores = jnp.concatenate([near_scores[h], dot(q_h, k_h, NT) + far_bias], axis=1)
        peak = jnp.max(scores, axis=1, keepdims=True)
        powers = jnp.exp((scores - peak) * scale)
        prob = powers * (1.0 / jnp.sum(powers, axis=1, keepdims=True))
        dprobs = jnp.concatenate([near_dprobs[h], dot(g_h, values[far_rows, cols], NT)], axis=1)
        delta = jnp.sum(prob * dprobs, axis=1, keepdims=True)
        prob_bf = prob.astype(BF16)
        dscore = (prob * (dprobs - delta) * scale).astype(BF16)
        probs[h] = prob_bf
        dscores[h] = dscore
        dk = dot(dscore[:, 2 * TOK :], q_h, TN)
        pk[far_rows, cols] = dk[:, :128].astype(BF16)
        rope_sum = rope_sum + dk[:, 128:]
        pv[far_rows, cols] = dot(prob_bf[:, 2 * TOK :], g_h, TN).astype(BF16)
    share[2] = jnp.zeros((WIRE, 128), BF16)

    def lifted(part, tokens):
        grad = dot(ku_ref[part, :], pk[tokens, :], NT)
        return grad + dot(vu_ref[part, :], pv[tokens, :], NT)

    for i in (1, 2, 0):
        begin, end = PARTS[i][0], PARTS[i][0] + PARTS[i][1]
        grad = lifted(slice(begin, min(end, LATENT)), far_rows)
        for j in range(2):
            share[j, begin : min(end, LATENT), :] = grad[:, j * TOK : (j + 1) * TOK].astype(BF16)
            if i == 0:
                turned = rope_sum[j * TOK : (j + 1) * TOK].T
                share[j, LATENT:, :] = turned[:ROPE].astype(BF16)
        for level in (7, 6, 5, 4, 3, 2):
            pieces[level - 1, begin:end, :] = share[slot_of[level], begin:end, :]
        if i > 0:
            ex.start(("back", i))
            ex.start(("four", i))
        else:
            ex.start(("eight", 0))
    for k in (2, 1):
        ex.start(("near", k))

    def piece(level, part):
        return pieces[level - 1, part[0] : part[0] + part[1], :].astype(F32)

    def got(ref, part, valid):
        return jnp.where(valid, ref[part[0] : part[0] + part[1], :].astype(F32), 0.0)

    near_rows = slice(0, 2 * TOK)
    rope_sum = jnp.zeros((2 * TOK, 128), F32)
    for h in range(HEADS):
        cols = slice(h * 128, (h + 1) * 128)
        dk = dot(dscores[h, :, : 2 * TOK], qa[:, h * 256 : (h + 1) * 256], TN)
        pk[near_rows, cols] = dk[:, :128].astype(BF16)
        rope_sum = rope_sum + dk[:, 128:]
        pv[near_rows, cols] = dot(probs[h, :, : 2 * TOK], og_ref[:, cols], TN).astype(BF16)
    grad = lifted(slice(0, LATENT), near_rows)
    own_grad[:LATENT, :] = grad[:, :TOK]
    own_grad[LATENT:, :] = rope_sum[:TOK].T[:ROPE]
    pieces[0, :LATENT, :] = grad[:, TOK:].astype(BF16)
    pieces[0, LATENT:, :] = rope_sum[TOK:].T[:ROPE].astype(BF16)
    ex.start(("near", 0))

    ex.wait(("eight", 0))
    a0, a1 = PART_A[0], PART_A[0] + PART_A[1]
    t4[a0:a1, :] = (piece(6, PART_A) + jnp.where(z <= 11, r8[...].astype(F32), 0.0)).astype(BF16)
    ex.start(("four", 0))
    for i in (1, 2):
        ex.wait(("back", i))
        ex.start(("on", i))

    def forward_out(h):
        cols = slice(h * 128, (h + 1) * 128)
        base = h * (NOPE + ROPE)
        att_ref[:, cols] = dot(probs[h], values[:, cols]).astype(BF16)
        k_h = jnp.concatenate([keys[:, cols], rope[...]], axis=1)
        gq_ref[:, base : base + 192] = dot(dscores[h], k_h)[:, :192].astype(BF16)

    for i in (1, 2, 0):
        part = PARTS[i]
        ex.wait(("four", i))
        t2[part[0] : part[0] + part[1], :] = (
            piece(5, part) + got(r4, part, z <= 13)
        ).astype(BF16)
        ex.start(("two", i))
    for h in range(4):
        forward_out(h)
    for k in range(3):
        ex.wait(("near", k))
    for i in (1, 2, 0):
        part = PARTS[i]
        ex.wait(("two", i))
        total = piece(4, part) + got(r2, part, z <= 14)
        for k in range(3):
            total = total + got(near.at[k], part, y + 2**k >= NY)
        t1[part[0] : part[0] + part[1], :] = total.astype(BF16)
        ex.start(("one", i))
    for h in range(4, HEADS):
        forward_out(h)
    for i in (1, 2):
        ex.wait(("on", i))
    for i in (1, 2, 0):
        part = PARTS[i]
        ex.wait(("one", i))
        total = own_grad[part[0] : part[0] + part[1], :] + got(r1, part, z <= 14)
        for k in range(3):
            total = total + got(near.at[k], part, y + 2**k < NY)
        if i > 0:
            total = total + got(far, part, z < 8)
        gl_ref[part[0] : part[0] + part[1], :] = total.astype(BF16)
    ex.finish()


def on_device(queries, latents, key_up, value_up, link_mask, out_grad):
    vmem = pl.BlockSpec(memory_space=pltpu.VMEM)
    hbm = pl.BlockSpec(memory_space=pltpu.HBM)
    block = pltpu.VMEM((WIRE, 128), BF16)
    keyed = pltpu.VMEM((SLOTS * TOK, WIDTH), BF16)
    passed = pltpu.VMEM((2, 192, 128), BF16)
    attention, grad_queries, grad_latents = pl.pallas_call(
        kernel,
        out_shape=(
            jax.ShapeDtypeStruct((TOK, WIDTH), BF16),
            jax.ShapeDtypeStruct((TOK, HEADS * (NOPE + ROPE)), BF16),
            jax.ShapeDtypeStruct((WIRE, TOK), BF16),
        ),
        in_specs=[pl.BlockSpec(memory_space=pltpu.SMEM)] + [hbm] * 5,
        out_specs=(vmem,) * 3,
        scratch_shapes=[
            pltpu.VMEM((TOK, HEADS * (NOPE + ROPE)), BF16),
            pltpu.VMEM((LATENT, WIDTH), BF16),
            pltpu.VMEM((LATENT, WIDTH), BF16),
            pltpu.VMEM((TOK, WIDTH), BF16),
            pltpu.VMEM((LEVELS, WIRE, 128), BF16),
            passed,
            pltpu.VMEM((TOK, HEADS * 256), BF16),
            keyed,
            keyed,
            pltpu.VMEM((SLOTS * TOK, 128), BF16),
            pltpu.VMEM((HEADS, TOK, 2 * TOK), F32),
            pltpu.VMEM((HEADS, TOK, 2 * TOK), F32),
            pltpu.VMEM((HEADS, TOK, 4 * TOK), BF16),
            pltpu.VMEM((HEADS, TOK, 4 * TOK), BF16),
            keyed,
            keyed,
            pltpu.VMEM((3, WIRE, 128), BF16),
            pltpu.VMEM((LEVELS - 1, WIRE, 128), BF16),
            pltpu.VMEM((WIRE, 128), F32),
            pltpu.VMEM((192, 128), BF16),
            block, block, block, block, block, block,
            passed,
            block,
            pltpu.VMEM((3, WIRE, 128), BF16),
            pltpu.SemaphoreType.DMA((5,)),
            pltpu.SemaphoreType.DMA((MOVES,)),
            pltpu.SemaphoreType.DMA((MOVES,)),
        ],
        compiler_params=pltpu.CompilerParams(
            collective_id=0, has_side_effects=True, vmem_limit_bytes=60 * 2**20
        ),
        name="attend",
    )(link_mask, queries, latents.T, key_up, value_up, out_grad)
    return attention, grad_queries, grad_latents.T


def solution(mesh):
    split = P(("dp", "ctx"), None)
    return jax.shard_map(
        on_device,
        mesh=mesh,
        in_specs=(split, split, P(), P(), split, split),
        out_specs=(split, split, split),
        check_vma=False,
    )
```

time: 84.8 us -> 80.8 us (0.953)
  the two profiles are of different devices: /device:TPU:6 before, /device:TPU:64 now
where the time goes in v2:
time: 80.8 us; the launch traced here: 80.7 us
  Pallas kernels  76.6 us (95%)
  local copies, waits for them, and re-layouts  3.41 us (4%)
    pallas_call x1, Pallas kernels, on_device(): pl.pallas_call(kernel, out_shape=(jax.ShapeDtypeStruct((TOK, WIDTH), BF16...  76.6 us
    unnamed x7, local copies, waits for them, and re-layouts  3.41 us

profile of v2, /device:TPU:64, one launch (start us, length us, event | category | flops | bytes accessed | tf_op | source)
XLA Modules:
  0.0 80.7 jit_solution(10407895595941225862)
XLA Ops:
  0.6 76.6 %attend.1 = (bf16[128,1024]{1,0:T(8,128)(2,1)}, bf16[128,1536]{1,0:T(8,128)(2,1)}, bf16[576,128]{1,0:T(8,128)(2,1)}) custom-call(s32[1,128]{1,0:T(1,128)} %mask_ref.1, bf16[128,1536]{1,0:T(8,128)(2,1)} %q_hbm.1, bf16[576,128]{1,0:T(8,128)(2,1)} %bitcast.2, bf16[512,1024]{1,0:T(8,128)(2,1)} %ku_hbm.1, bf16[512,1024]{1,0:T(8,128)(2,1)} %vu_hbm.1, ...), custom_call_target="tpu_custom_call" | custom-call | tf_op jit(solution)/shard_map/attend/pallas_call | solution.py:395
  77.2 0.0 copy-start
  77.2 1.7 %copy.12 = bf16[128,1024]{1,0:T(8,128)(2,1)} copy(bf16[128,1024]{1,0:T(8,128)(2,1)} %get-tuple-element.12) | data formatting | bytes 524288
  79.0 0.0 copy-done
  79.0 0.0 copy-start.1
  79.0 0.7 copy.13
  79.7 0.3 copy-done.1
  80.0 0.7 copy.14
Async XLA Ops:
  77.2 1.7 %copy-start = (bf16[128,1536]{1,0:T(8,128)(2,1)S(1)}, bf16[128,1536]{1,0:T(8,128)(2,1)}, u32[]{:S(2)}) copy-start(bf16[128,1536]{1,0:T(8,128)(2,1)} %get-tuple-element.13) | copy-start | bytes 1179652
  79.0 1.0 %copy-start.1 = (bf16[576,128]{1,0:T(8,128)(2,1)S(1)}, bf16[576,128]{1,0:T(8,128)(2,1)}, u32[]{:S(2)}) copy-start(bf16[576,128]{1,0:T(8,128)(2,1)} %get-tuple-element.8) | copy-start | bytes 442372

commit v3 on v2

--- a/solution.py
+++ b/solution.py
@@ -122,9 +122,11 @@
     for k in range(3):
         by = 2**k
         moves["out near", k] = Move(own, cand.at[k + 1], 0, by, lambda z, y, by=by: y + by < NY)
-        moves["out cross", k] = Move(
-            cand.at[4], cand.at[k + 1], 0, by, lambda z, y, by=by: (y + by >= NY) & (z >= 1)
-        )
+        for i, part in enumerate(PARTS):
+            moves["out cross", k, i] = Move(
+                rows(cand, part, 4), rows(cand, part, k + 1), 0, by,
+                lambda z, y, by=by: (y + by >= NY) & (z >= 1),
+            )
     return moves
 
 
@@ -151,7 +153,7 @@
     return moves
 
 
-MOVES = 20 + 17
+MOVES = 26 + 17
 NT = (((1,), (1,)), ((), ()))
 TN = (((0,), (0,)), ((), ()))
 
@@ -163,7 +165,7 @@
 def kernel(
     mask_ref, q_hbm, lat_hbm, ku_hbm, vu_hbm, og_hbm, att_ref, gq_ref, gl_ref,
     q_ref, ku_ref, vu_ref, og_ref, cand, out_passed,
-    qa, keys, values, rope, near_scores, near_dprobs, probs, dscores, pk, pv,
+    qa, keys, values, rope, near_powers, near_dprobs, near_peak, near_sum, near_dot, probs, dscores, pk, pv,
     share, pieces, own_grad, r8, r4, r2, r1, t4, t2, t1, passed, far, near,
     local_sem, send_sem, recv_sem,
 ):
@@ -218,16 +220,26 @@
         cols = slice(h * 128, (h + 1) * 128)
         k_h = jnp.concatenate([keys[: 2 * TOK, cols], rope[: 2 * TOK, :]], axis=1)
         scores = dot(qa[:, h * 256 : (h + 1) * 256], k_h, NT)
-        near_scores[h] = jnp.where(near_allowed, scores, no)
-        near_dprobs[h] = dot(og_ref[:, cols], values[: 2 * TOK, cols], NT)
+        scores = jnp.where(near_allowed, scores, no)
+        peak = jnp.max(scores, axis=1, keepdims=True)
+        powers = jnp.exp((scores - peak) * scale)
+        dprobs = dot(og_ref[:, cols], values[: 2 * TOK, cols], NT)
+        near_powers[h] = powers
+        near_dprobs[h] = dprobs
+        near_peak[h] = peak
+        near_sum[h] = jnp.sum(powers, axis=1, keepdims=True)
+        near_dot[h] = jnp.sum(powers * dprobs, axis=1, keepdims=True)
+
+    def from_y(k):
+        ex.wait(("out near", k))
+        for i in range(3):
+            ex.wait(("out cross", k, i))
 
     ex.barrier()
     for i in (1, 2):
         ex.start(("out back", i))
     for i in range(3):
         ex.start(("out one", i))
-    for k in (2, 1, 0):
-        ex.start(("out near", k))
     local["q"].wait()
     for h in range(HEADS):
         base = h * (NOPE + ROPE)
@@ -237,8 +249,10 @@
     for i in range(3):
         ex.wait(("out one", i))
         ex.start(("out two", i))
-    for k in (2, 1, 0):
-        ex.start(("out cross", k))
+        for k in (2, 1, 0):
+            ex.start(("out cross", k, i))
+    for k in (0, 2, 1):
+        ex.start(("out near", k))
     for name in ("own", "ku", "vu", "og"):
         local[name].wait()
     project(0, cand[0, :LATENT])
@@ -249,19 +263,17 @@
     for i in range(3):
         ex.wait(("out two", i))
         ex.start(("out four", i))
-    ex.wait(("out near", 0))
-    ex.wait(("out cross", 0))
+    ex.wait(("out four", 0))
+    ex.start(("out eight", 0))
+    from_y(0)
     project(1, cand[1, :LATENT])
     rope_rows(1, cand[1, LATENT:])
-    ex.wait(("out four", 0))
-    ex.start(("out eight", 0))
     for h in range(HEADS):
         near_head(h)
     for i in (1, 2):
         ex.wait(("out four", i))
     for k in (1, 2):
-        ex.wait(("out near", k))
-        ex.wait(("out cross", k))
+        from_y(k)
     ex.wait(("out eight", 0))
     for i in (1, 2):
         ex.wait(("out on", i))
@@ -277,20 +289,25 @@
         q_h = qa[:, h * 256 : (h + 1) * 256]
         g_h = og_ref[:, cols]
         k_h = jnp.concatenate([keys[far_rows, cols], rope[far_rows, :]], axis=1)
-        scores = jnp.concatenate([near_scores[h], dot(q_h, k_h, NT) + far_bias], axis=1)
-        peak = jnp.max(scores, axis=1, keepdims=True)
+        scores = dot(q_h, k_h, NT) + far_bias
+        peak = jnp.maximum(near_peak[h], jnp.max(scores, axis=1, keepdims=True))
         powers = jnp.exp((scores - peak) * scale)
-        prob = powers * (1.0 / jnp.sum(powers, axis=1, keepdims=True))
-        dprobs = jnp.concatenate([near_dprobs[h], dot(g_h, values[far_rows, cols], NT)], axis=1)
-        delta = jnp.sum(prob * dprobs, axis=1, keepdims=True)
+        near_factor = jnp.exp((near_peak[h] - peak) * scale)
+        inverse = 1.0 / (near_factor * near_sum[h] + jnp.sum(powers, axis=1, keepdims=True))
+        near_factor = near_factor * inverse
+        prob = powers * inverse
+        dprobs = dot(g_h, values[far_rows, cols], NT)
+        delta = near_factor * near_dot[h] + jnp.sum(prob * dprobs, axis=1, keepdims=True)
         prob_bf = prob.astype(BF16)
         dscore = (prob * (dprobs - delta) * scale).astype(BF16)
-        probs[h] = prob_bf
-        dscores[h] = dscore
-        dk = dot(dscore[:, 2 * TOK :], q_h, TN)
+        probs[h, :, 2 * TOK :] = prob_bf
+        dscores[h, :, 2 * TOK :] = dscore
+        near_sum[h] = near_factor
+        near_dot[h] = delta
+        dk = dot(dscore, q_h, TN)
         pk[far_rows, cols] = dk[:, :128].astype(BF16)
         rope_sum = rope_sum + dk[:, 128:]
-        pv[far_rows, cols] = dot(prob_bf[:, 2 * TOK :], g_h, TN).astype(BF16)
+        pv[far_rows, cols] = dot(prob_bf, g_h, TN).astype(BF16)
     share[2] = jnp.zeros((WIRE, 128), BF16)
 
     def lifted(part, tokens):
@@ -325,10 +342,15 @@
     rope_sum = jnp.zeros((2 * TOK, 128), F32)
     for h in range(HEADS):
         cols = slice(h * 128, (h + 1) * 128)
-        dk = dot(dscores[h, :, : 2 * TOK], qa[:, h * 256 : (h + 1) * 256], TN)
+        prob = near_powers[h] * near_sum[h]
+        prob_bf = prob.astype(BF16)
+        dscore = (prob * (near_dprobs[h] - near_dot[h]) * scale).astype(BF16)
+        probs[h, :, : 2 * TOK] = prob_bf
+        dscores[h, :, : 2 * TOK] = dscore
+        dk = dot(dscore, qa[:, h * 256 : (h + 1) * 256], TN)
         pk[near_rows, cols] = dk[:, :128].astype(BF16)
         rope_sum = rope_sum + dk[:, 128:]
-        pv[near_rows, cols] = dot(probs[h, :, : 2 * TOK], og_ref[:, cols], TN).astype(BF16)
+        pv[near_rows, cols] = dot(prob_bf, og_ref[:, cols], TN).astype(BF16)
     grad = lifted(slice(0, LATENT), near_rows)
     own_grad[:LATENT, :] = grad[:, :TOK]
     own_grad[LATENT:, :] = rope_sum[:TOK].T[:ROPE]
@@ -386,6 +408,32 @@
     ex.finish()
 
 
+def hand_over_kernel(*refs):
+    sources, targets, held, sem = refs[:3], refs[3:6], refs[6:9], refs[9]
+    into = [pltpu.make_async_copy(sources[i], held[i], sem.at[i]) for i in range(3)]
+    out = [pltpu.make_async_copy(held[i], targets[i], sem.at[3 + i]) for i in range(3)]
+    for copy in into:
+        copy.start()
+    for i in range(3):
+        into[i].wait()
+        out[i].start()
+    for copy in out:
+        copy.wait()
+
+
+def hand_over(*arrays):
+    hbm = pl.BlockSpec(memory_space=pltpu.HBM)
+    return pl.pallas_call(
+        hand_over_kernel,
+        out_shape=tuple(jax.ShapeDtypeStruct(a.shape, a.dtype) for a in arrays),
+        in_specs=[hbm] * 3,
+        out_specs=(hbm,) * 3,
+        scratch_shapes=[pltpu.VMEM(a.shape, a.dtype) for a in arrays] + [pltpu.SemaphoreType.DMA((6,))],
+        compiler_params=pltpu.CompilerParams(vmem_limit_bytes=60 * 2**20),
+        name="hand_over",
+    )(*arrays)
+
+
 def on_device(queries, latents, key_up, value_up, link_mask, out_grad):
     vmem = pl.BlockSpec(memory_space=pltpu.VMEM)
     hbm = pl.BlockSpec(memory_space=pltpu.HBM)
@@ -414,6 +462,9 @@
             pltpu.VMEM((SLOTS * TOK, 128), BF16),
             pltpu.VMEM((HEADS, TOK, 2 * TOK), F32),
             pltpu.VMEM((HEADS, TOK, 2 * TOK), F32),
+            pltpu.VMEM((HEADS, TOK, 1), F32),
+            pltpu.VMEM((HEADS, TOK, 1), F32),
+            pltpu.VMEM((HEADS, TOK, 1), F32),
             pltpu.VMEM((HEADS, TOK, 4 * TOK), BF16),
             pltpu.VMEM((HEADS, TOK, 4 * TOK), BF16),
             keyed,
@@ -435,6 +486,7 @@
         ),
         name="attend",
     )(link_mask, queries, latents.T, key_up, value_up, out_grad)
+    attention, grad_queries, grad_latents = hand_over(attention, grad_queries, grad_latents)
     return attention, grad_queries, grad_latents.T
 
 

time: 80.8 us -> 75.8 us (0.938)
  the two profiles are of different devices: /device:TPU:64 before, /device:TPU:6 now
where the time goes in v3:
time: 75.8 us; the launch traced here: 75.6 us
  Pallas kernels  74.9 us (99%)
    pallas_call x1, Pallas kernels, on_device(): pl.pallas_call(kernel, out_shape=(jax.ShapeDtypeStruct((TOK, WIDTH), BF16...  73 us
    pallas_call x1, Pallas kernels, hand_over(): pl.pallas_call(hand_over_kernel, out_shape=tuple((jax.ShapeDtypeStruct(a....  1.92 us

profile of v3, /device:TPU:6, one launch (start us, length us, event | category | flops | bytes accessed | tf_op | source)
XLA Modules:
  0.0 75.6 jit_solution(16789815623846061894)
XLA Ops:
  0.6 73.0 %attend.1 = (bf16[128,1024]{1,0:T(8,128)(2,1)}, bf16[128,1536]{1,0:T(8,128)(2,1)}, bf16[576,128]{1,0:T(8,128)(2,1)}) custom-call(s32[1,128]{1,0:T(1,128)} %mask_ref.1, bf16[128,1536]{1,0:T(8,128)(2,1)} %q_hbm.1, bf16[576,128]{1,0:T(8,128)(2,1)} %bitcast.2, bf16[512,1024]{1,0:T(8,128)(2,1)} %ku_hbm.1, bf16[512,1024]{1,0:T(8,128)(2,1)} %vu_hbm.1, ...), custom_call_target="tpu_custom_call" | custom-call | tf_op jit(solution)/shard_map/attend/pallas_call | solution.py:443
  73.7 1.9 %hand_over.1 = (bf16[128,1024]{1,0:T(8,128)(2,1)}, bf16[128,1536]{1,0:T(8,128)(2,1)}, bf16[576,128]{1,0:T(8,128)(2,1)}) custom-call(bf16[128,1024]{1,0:T(8,128)(2,1)} %get-tuple-element.9.refs_0_, bf16[128,1536]{1,0:T(8,128)(2,1)} %get-tuple-element.10.refs_1_, bf16[576,128]{1,0:T(8,128)(2,1)} %get-tuple-element.11.refs_2_), custom_call_target="tpu_custom_call" | custom-call | tf_op jit(solution)/shard_map/hand_over/pallas_call | solution.py:426

commit v4 on v3

--- a/solution.py
+++ b/solution.py
@@ -130,7 +130,7 @@
     return moves
 
 
-def homeward_moves(pieces, r8, r4, r2, r1, t4, t2, t1, passed, far, near):
+def homeward_moves(pieces, r8, r4, r2, r1, t4, t2, t1, passed, far, near, cross):
     moves = {}
     for i, part in enumerate(PARTS):
         p7 = rows(pieces, part, 6)
@@ -148,12 +148,15 @@
     for k in range(3):
         by = 2**k
         moves["near", k] = Move(
-            pieces.at[k], near.at[k], 0, -by, lambda z, y, by=by: (y >= by) | (z >= 1)
+            pieces.at[k], near.at[k], 0, -by, lambda z, y, by=by: y >= by
+        )
+        moves["cross", k] = Move(
+            pieces.at[k], cross.at[k], 0, -by, lambda z, y, by=by: (y < by) & (z >= 1)
         )
     return moves
 
 
-MOVES = 26 + 17
+MOVES = 26 + 20
 NT = (((1,), (1,)), ((), ()))
 TN = (((0,), (0,)), ((), ()))
 
@@ -166,11 +169,11 @@
     mask_ref, q_hbm, lat_hbm, ku_hbm, vu_hbm, og_hbm, att_ref, gq_ref, gl_ref,
     q_ref, ku_ref, vu_ref, og_ref, cand, out_passed,
     qa, keys, values, rope, near_powers, near_dprobs, near_peak, near_sum, near_dot, probs, dscores, pk, pv,
-    share, pieces, own_grad, r8, r4, r2, r1, t4, t2, t1, passed, far, near,
+    share, pieces, own_grad, r8, r4, r2, r1, t4, t2, t1, passed, far, near, cross,
     local_sem, send_sem, recv_sem,
 ):
     moves = outward_moves(lat_hbm, cand, out_passed)
-    moves.update(homeward_moves(pieces, r8, r4, r2, r1, t4, t2, t1, passed, far, near))
+    moves.update(homeward_moves(pieces, r8, r4, r2, r1, t4, t2, t1, passed, far, near, cross))
     ex = Exchange(moves, send_sem, recv_sem)
     z, y = ex.z, ex.y
     local = {
@@ -330,6 +333,7 @@
         else:
             ex.start(("eight", 0))
     for k in (2, 1):
+        ex.start(("cross", k))
         ex.start(("near", k))
 
     def piece(level, part):
@@ -356,6 +360,7 @@
     own_grad[LATENT:, :] = rope_sum[:TOK].T[:ROPE]
     pieces[0, :LATENT, :] = grad[:, TOK:].astype(BF16)
     pieces[0, LATENT:, :] = rope_sum[TOK:].T[:ROPE].astype(BF16)
+    ex.start(("cross", 0))
     ex.start(("near", 0))
 
     ex.wait(("eight", 0))
@@ -383,17 +388,19 @@
     for h in range(4):
         forward_out(h)
     for k in range(3):
-        ex.wait(("near", k))
+        ex.wait(("cross", k))
     for i in (1, 2, 0):
         part = PARTS[i]
         ex.wait(("two", i))
         total = piece(4, part) + got(r2, part, z <= 14)
         for k in range(3):
-            total = total + got(near.at[k], part, y + 2**k >= NY)
+            total = total + got(cross.at[k], part, (y + 2**k >= NY) & (z >= 1))
         t1[part[0] : part[0] + part[1], :] = total.astype(BF16)
         ex.start(("one", i))
     for h in range(4, HEADS):
         forward_out(h)
+    for k in range(3):
+        ex.wait(("near", k))
     for i in (1, 2):
         ex.wait(("on", i))
     for i in (1, 2, 0):
@@ -477,6 +484,7 @@
             passed,
             block,
             pltpu.VMEM((3, WIRE, 128), BF16),
+            pltpu.VMEM((3, WIRE, 128), BF16),
             pltpu.SemaphoreType.DMA((5,)),
             pltpu.SemaphoreType.DMA((MOVES,)),
             pltpu.SemaphoreType.DMA((MOVES,)),

time: 75.8 us -> 75.8 us (level)
  no operation moved by 1% of the time
where the time goes in v4:
time: 75.8 us; the launch traced here: 75.7 us
  Pallas kernels  75 us (99%)
    pallas_call x1, Pallas kernels, on_device(): pl.pallas_call(kernel, out_shape=(jax.ShapeDtypeStruct((TOK, WIDTH), BF16...  73.1 us
    pallas_call x1, Pallas kernels, hand_over(): pl.pallas_call(hand_over_kernel, out_shape=tuple((jax.ShapeDtypeStruct(a....  1.92 us

profile of v4, /device:TPU:6, one launch (start us, length us, event | category | flops | bytes accessed | tf_op | source)
XLA Modules:
  0.0 75.7 jit_solution(507665592090412341)
XLA Ops:
  0.6 73.1 %attend.1 = (bf16[128,1024]{1,0:T(8,128)(2,1)}, bf16[128,1536]{1,0:T(8,128)(2,1)}, bf16[576,128]{1,0:T(8,128)(2,1)}) custom-call(s32[1,128]{1,0:T(1,128)} %mask_ref.1, bf16[128,1536]{1,0:T(8,128)(2,1)} %q_hbm.1, bf16[576,128]{1,0:T(8,128)(2,1)} %bitcast.2, bf16[512,1024]{1,0:T(8,128)(2,1)} %ku_hbm.1, bf16[512,1024]{1,0:T(8,128)(2,1)} %vu_hbm.1, ...), custom_call_target="tpu_custom_call" | custom-call | tf_op jit(solution)/shard_map/attend/pallas_call | solution.py:450
  73.7 1.9 %hand_over.1 = (bf16[128,1024]{1,0:T(8,128)(2,1)}, bf16[128,1536]{1,0:T(8,128)(2,1)}, bf16[576,128]{1,0:T(8,128)(2,1)}) custom-call(bf16[128,1024]{1,0:T(8,128)(2,1)} %get-tuple-element.9.refs_0_, bf16[128,1536]{1,0:T(8,128)(2,1)} %get-tuple-element.10.refs_1_, bf16[576,128]{1,0:T(8,128)(2,1)} %get-tuple-element.11.refs_2_), custom_call_target="tpu_custom_call" | custom-call | tf_op jit(solution)/shard_map/hand_over/pallas_call | solution.py:433

commit v5 on v3

--- a/solution.py
+++ b/solution.py
@@ -314,7 +314,7 @@
         grad = dot(ku_ref[part, :], pk[tokens, :], NT)
         return grad + dot(vu_ref[part, :], pv[tokens, :], NT)
 
-    for i in (1, 2, 0):
+    for i in (0, 1, 2):
         begin, end = PARTS[i][0], PARTS[i][0] + PARTS[i][1]
         grad = lifted(slice(begin, min(end, LATENT)), far_rows)
         for j in range(2):
@@ -380,8 +380,6 @@
             piece(5, part) + got(r4, part, z <= 13)
         ).astype(BF16)
         ex.start(("two", i))
-    for h in range(4):
-        forward_out(h)
     for k in range(3):
         ex.wait(("near", k))
     for i in (1, 2, 0):
@@ -392,7 +390,7 @@
             total = total + got(near.at[k], part, y + 2**k >= NY)
         t1[part[0] : part[0] + part[1], :] = total.astype(BF16)
         ex.start(("one", i))
-    for h in range(4, HEADS):
+    for h in range(HEADS):
         forward_out(h)
     for i in (1, 2):
         ex.wait(("on", i))

time: 75.8 us -> 75.2 us (level)
  the two profiles are of different devices: /device:TPU:6 before, /device:TPU:68 now
where the time goes in v5:
time: 75.2 us; the launch traced here: 75.1 us
  Pallas kernels  74.4 us (99%)
    pallas_call x1, Pallas kernels, on_device(): pl.pallas_call(kernel, out_shape=(jax.ShapeDtypeStruct((TOK, WIDTH), BF16...  72.5 us
    pallas_call x1, Pallas kernels, hand_over(): pl.pallas_call(hand_over_kernel, out_shape=tuple((jax.ShapeDtypeStruct(a....  1.92 us

profile of v5, /device:TPU:68, one launch (start us, length us, event | category | flops | bytes accessed | tf_op | source)
XLA Modules:
  0.0 75.1 jit_solution(356463439313349525)
XLA Ops:
  0.6 72.5 %attend.1 = (bf16[128,1024]{1,0:T(8,128)(2,1)}, bf16[128,1536]{1,0:T(8,128)(2,1)}, bf16[576,128]{1,0:T(8,128)(2,1)}) custom-call(s32[1,128]{1,0:T(1,128)} %mask_ref.1, bf16[128,1536]{1,0:T(8,128)(2,1)} %q_hbm.1, bf16[576,128]{1,0:T(8,128)(2,1)} %bitcast.2, bf16[512,1024]{1,0:T(8,128)(2,1)} %ku_hbm.1, bf16[512,1024]{1,0:T(8,128)(2,1)} %vu_hbm.1, ...), custom_call_target="tpu_custom_call" | custom-call | tf_op jit(solution)/shard_map/attend/pallas_call | solution.py:441
  73.1 1.9 %hand_over.1 = (bf16[128,1024]{1,0:T(8,128)(2,1)}, bf16[128,1536]{1,0:T(8,128)(2,1)}, bf16[576,128]{1,0:T(8,128)(2,1)}) custom-call(bf16[128,1024]{1,0:T(8,128)(2,1)} %get-tuple-element.9.refs_0_, bf16[128,1536]{1,0:T(8,128)(2,1)} %get-tuple-element.10.refs_1_, bf16[576,128]{1,0:T(8,128)(2,1)} %get-tuple-element.11.refs_2_), custom_call_target="tpu_custom_call" | custom-call | tf_op jit(solution)/shard_map/hand_over/pallas_call | solution.py:424
